TPU v7x, 128 devices: a whole 4x4x4 slice. The times are simulated.
128 devices in a mesh: seqhi: 4 (over y), seqlo: 32 (over z, x, core).
Axes of the slice: x: 4, y: 4, z: 4, core: 2. Of those that a mesh axis runs over, the one named last changes fastest.
Arguments:
- query: bfloat16 [32768, 1280], P(('seqhi', 'seqlo')), may hold values from -6 to 6
- key: bfloat16 [32768, 1280], P(('seqhi', 'seqlo')), may hold values from -6 to 6
- value: bfloat16 [32768, 1280], P(('seqhi', 'seqlo')), may hold values from -6 to 6
- grad_out: bfloat16 [32768, 1280], P(('seqhi', 'seqlo')), may hold values from -6 to 6
- offsets: int32 [3, 10], replicated, may hold values from 0 to 63, as said below
Outputs:
- attended: bfloat16 [32768, 1280], P(('seqhi', 'seqlo'))
- grad_query: bfloat16 [32768, 1280], P(('seqhi', 'seqlo'))
- grad_key: bfloat16 [32768, 1280], P(('seqhi', 'seqlo'))
- grad_value: bfloat16 [32768, 1280], P(('seqhi', 'seqlo'))
Inputs may be any that keep to these rules, and one draw needn't show every extreme that they name: offsets[l, h] is below 2^(3 * l); at every level some head has offset 2^(3 * l) - 1.
All inputs are finite; a program needn't handle non-finite values.
Results may differ from a plain program's by a relative error of at most 0.0096.
Values may be sent and summed in bfloat16 or wider, within the bound.
No kernel may reach another device: no remote copies, remote signals or barrier semaphores. Data moves between devices by JAX's collectives and lax.ppermute only.
A program may use at most 192 MiB of HBM per device.

v0:
```python
import jax
import jax.numpy as jnp
from jax import lax
from jax.sharding import PartitionSpec as P

H = 10
HD = 128
SEG0 = 1024
SKIP = 3
LEVELS = 3


def swapped(x, axis, distance):
    return lax.ppermute(x, axis, [(i, i ^ 1 << distance) for i in range(lax.axis_size(axis))])


def pick(source, shifts, stride):
    row_count = source.shape[0]
    grouped = source.reshape((row_count // stride, stride) + source.shape[1:])
    chosen = jnp.arange(stride)[:, None] == shifts[None, :]
    chosen = chosen.reshape((1, stride, shifts.shape[0]) + (1,) * (source.ndim - 2))
    picked = jnp.sum(jnp.where(chosen, grouped, jnp.zeros((), source.dtype)), axis=1)
    return jnp.moveaxis(picked, 1, 0)


def spread(values, shifts, stride, filler):
    lifted = jnp.moveaxis(values, 0, 1)
    count_rows = lifted.shape[0]
    chosen = jnp.arange(stride)[:, None] == shifts[None, :]
    chosen = chosen.reshape((1, stride, shifts.shape[0]) + (1,) * (lifted.ndim - 2))
    placed = jnp.where(chosen, lifted[:, None], filler)
    return placed.reshape((count_rows * stride,) + lifted.shape[1:])


def scores_of(sel_query, sel_key, scaling):
    return (
        jnp.einsum("hsid,hsjd->hsij", sel_query, sel_key, preferred_element_type=jnp.float32)
        * scaling
    )


def bit_counts(groups, count_lo):
    lo_bits = min(groups, count_lo).bit_length() - 1
    hi_bits = (groups // count_lo).bit_length() - 1 if groups > count_lo else 0
    return (lo_bits, hi_bits)


def lo_doubling(pair_rows, lo_bits):
    for bit_id in range(lo_bits):
        partner = swapped(pair_rows, "seqlo", bit_id)
        is_lower = lax.axis_index("seqlo") >> bit_id & 1 == 0
        pair_rows = jnp.where(
            is_lower,
            jnp.concatenate([pair_rows, partner], 2),
            jnp.concatenate([partner, pair_rows], 2),
        )
    return pair_rows


def fetch(pair_rows, groups, count_lo):
    lo_bits, hi_bits = bit_counts(groups, count_lo)
    pair_rows = lo_doubling(pair_rows, lo_bits)
    for bit_id in range(hi_bits):
        partner = swapped(pair_rows, "seqhi", bit_id)
        is_lower = lax.axis_index("seqhi") >> bit_id & 1 == 0
        pair_rows = jnp.where(
            is_lower,
            jnp.concatenate([pair_rows, partner], 2),
            jnp.concatenate([partner, pair_rows], 2),
        )
    return pair_rows


def halve_step(partial_value, bit_on, received_fn):
    half_rows = partial_value.shape[2] // 2
    lower_half = partial_value[:, :, :half_rows]
    upper_half = partial_value[:, :, half_rows:]
    outgoing = jnp.where(bit_on, lower_half, upper_half)
    kept_half = jnp.where(bit_on, upper_half, lower_half)
    return kept_half + received_fn(outgoing)


def lo_halving(partial_value, lo_bits):
    for bit_id in reversed(range(lo_bits)):
        bit_on = lax.axis_index("seqlo") >> bit_id & 1 == 1
        partial_value = halve_step(
            partial_value, bit_on, lambda outgoing: swapped(outgoing, "seqlo", bit_id)
        )
    return partial_value


def give_back(partial_value, groups, count_lo):
    lo_bits, hi_bits = bit_counts(groups, count_lo)
    for bit_id in reversed(range(hi_bits)):
        bit_on = lax.axis_index("seqhi") >> bit_id & 1 == 1
        partial_value = halve_step(
            partial_value,
            bit_on,
            lambda outgoing: swapped(outgoing.astype(jnp.bfloat16), "seqhi", bit_id).astype(
                outgoing.dtype
            ),
        )
    return lo_halving(partial_value, lo_bits)


def body(query, key, value, grad_out, offsets):
    row_count = query.shape[0]
    count_lo = lax.axis_size("seqlo")
    total_tokens = row_count * count_lo * lax.axis_size("seqhi")
    scaling = HD ** (-0.5)
    query3 = query.reshape(row_count, H, HD)
    key3 = key.reshape(row_count, H, HD)
    value3 = value.reshape(row_count, H, HD)
    grad3 = grad_out.reshape(row_count, H, HD)
    levels = []
    for level_id in range(LEVELS):
        stride = 2 ** (SKIP * level_id)
        segment = min(SEG0 * stride, total_tokens)
        groups = max(1, segment // row_count)
        shifts = offsets[level_id]
        sel_query = pick(query3, shifts, stride)
        sel_grad = pick(grad3, shifts, stride)
        sel_key = pick(key3, shifts, stride)
        sel_value = pick(value3, shifts, stride)
        gathered = fetch(jnp.stack([sel_key, sel_value]), groups, count_lo)
        sel_key = gathered[0][:, None]
        sel_value = gathered[1][:, None]
        sel_query = sel_query[:, None]
        sel_grad = sel_grad[:, None]
        scores = scores_of(sel_query, sel_key, scaling)
        levels.append((stride, shifts, groups, sel_query, sel_key, sel_value, sel_grad, scores))
    peak_score = jnp.full((row_count, H), -jnp.inf, jnp.float32)
    for stride, shifts, groups, sel_query, sel_key, sel_value, sel_grad, scores in levels:
        peak_score = jnp.maximum(
            peak_score, spread(jnp.max(scores, -1).reshape(H, -1), shifts, stride, -jnp.inf)
        )
    total_exp = jnp.zeros((row_count, H), jnp.float32)
    for stride, shifts, groups, sel_query, sel_key, sel_value, sel_grad, scores in levels:
        peak_sel = pick(peak_score, shifts, stride).reshape(scores.shape[:3])
        total_exp = total_exp + spread(
            jnp.sum(jnp.exp(scores - peak_sel[..., None]), -1).reshape(H, -1), shifts, stride, 0.0
        )
    log_total = peak_score + jnp.log(total_exp)
    full_out = jnp.zeros((row_count, H, HD), jnp.float32)
    for stride, shifts, groups, sel_query, sel_key, sel_value, sel_grad, scores in levels:
        log_sel = pick(log_total, shifts, stride).reshape(scores.shape[:3])
        prob_b = jnp.exp(scores - log_sel[..., None]).astype(jnp.bfloat16)
        partial_value = jnp.einsum(
            "hsij,hsjd->hsid", prob_b, sel_value, preferred_element_type=jnp.float32
        )
        full_out = full_out + spread(partial_value.reshape(H, -1, HD), shifts, stride, 0.0)
    row_dot = jnp.sum(grad3.astype(jnp.float32) * full_out, -1)
    grad_query = jnp.zeros((row_count, H, HD), jnp.float32)
    grad_key = jnp.zeros((row_count, H, HD), jnp.float32)
    grad_value = jnp.zeros((row_count, H, HD), jnp.float32)
    for stride, shifts, groups, sel_query, sel_key, sel_value, sel_grad, scores in levels:
        log_sel = pick(log_total, shifts, stride).reshape(scores.shape[:3])
        dot_sel = pick(row_dot, shifts, stride).reshape(scores.shape[:3])
        prob = jnp.exp(scores - log_sel[..., None])
        prob_b = prob.astype(jnp.bfloat16)
        dprob = jnp.einsum(
            "hsid,hsjd->hsij", sel_grad, sel_value, preferred_element_type=jnp.float32
        )
        dscore = (prob * (dprob - dot_sel[..., None])).astype(jnp.bfloat16)
        query_part = (
            jnp.einsum("hsij,hsjd->hsid", dscore, sel_key, preferred_element_type=jnp.float32)
            * scaling
        )
        key_part = (
            jnp.einsum("hsij,hsid->hsjd", dscore, sel_query, preferred_element_type=jnp.float32)
            * scaling
        )
        value_part = jnp.einsum(
            "hsij,hsid->hsjd", prob_b, sel_grad, preferred_element_type=jnp.float32
        )
        grad_query = grad_query + spread(query_part.reshape(H, -1, HD), shifts, stride, 0.0)
        returned = give_back(jnp.stack([key_part[:, 0], value_part[:, 0]]), groups, count_lo)
        key_own = returned[0]
        value_own = returned[1]
        grad_key = grad_key + spread(key_own, shifts, stride, 0.0)
        grad_value = grad_value + spread(value_own, shifts, stride, 0.0)
    return (
        full_out.reshape(row_count, H * HD).astype(jnp.bfloat16),
        grad_query.reshape(row_count, H * HD).astype(jnp.bfloat16),
        grad_key.reshape(row_count, H * HD).astype(jnp.bfloat16),
        grad_value.reshape(row_count, H * HD).astype(jnp.bfloat16),
    )


def solution(mesh):
    return jax.shard_map(
        body,
        mesh=mesh,
        in_specs=(
            P(("seqhi", "seqlo"), None),
            P(("seqhi", "seqlo"), None),
            P(("seqhi", "seqlo"), None),
            P(("seqhi", "seqlo"), None),
            P(),
        ),
        out_specs=(
            P(("seqhi", "seqlo"), None),
            P(("seqhi", "seqlo"), None),
            P(("seqhi", "seqlo"), None),
            P(("seqhi", "seqlo"), None),
        ),
        check_vma=False,
    )
```

profile of v0, /device:TPU:1, one launch (start us, length us, event | category | flops | bytes accessed | tf_op | source)
XLA Modules:
  0.0 513.1 jit_solution(375923083082861420)
XLA Ops:
  23.0 7.1 %collective-permute-done.8 = bf16[2,10,8,128]{3,2,1,0:T(8,128)(2,1)S(1)} collective-permute-done((bf16[2,10,8,128]{3,2,1,0:T(8,128)(2,1)S(1)}, bf16[2,10,8,128]{3,2,1,0:T(8,128)(2,1)S(1)}, u32[]{:S(2)}, u32[]{:S(2)}) %collective-permute-start.8) | collective-permute-done | bytes 40992 | tf_op jit(solution)/shard_map/ppermute | solution.py:14
  44.6 4.9 collective-permute-done.4
  60.9 7.8 %collective-permute-done.12 = bf16[2,10,128,128]{3,2,1,0:T(8,128)(2,1)} collective-permute-done((bf16[2,10,128,128]{3,2,1,0:T(8,128)(2,1)}, bf16[2,10,128,128]{3,2,1,0:T(8,128)(2,1)}, u32[]{:S(2)}, u32[]{:S(2)}) %collective-permute-start.12) | collective-permute-done | bytes 655392 | tf_op jit(solution)/shard_map/ppermute | solution.py:14
  75.0 5.6 %collective-permute-done.5 = bf16[2,10,256,128]{3,2,1,0:T(8,128)(2,1)} collective-permute-done((bf16[2,10,256,128]{3,2,1,0:T(8,128)(2,1)}, bf16[2,10,256,128]{3,2,1,0:T(8,128)(2,1)}, u32[]{:S(2)}, u32[]{:S(2)}) %collective-permute-start.5) | collective-permute-done | bytes 1310752 | tf_op jit(solution)/shard_map/ppermute | solution.py:14
  80.7 4.3 maximum_select_fusion.3
  109.9 5.0 collective-permute-done.1
  114.9 4.2 maximum_select_fusion
  119.1 5.6 %multiply_reduce_fusion = (f32[10,256]{1,0:T(8,128)S(1)}, f32[10,256,1024]{2,1,0:T(8,128)}) fusion(bf16[2,10,1024,128]{3,2,1,0:T(8,128)(2,1)S(1)} %maximum_select_fusion, bf16[256,10,128]{2,0,1:T(8,128)(2,1)S(1)} %copy.95, pred[10]{0:T(512)(128)(4,1)S(1)} %copy-done.46), kind=kOutput, calls=%fused_computation.8 | convolution fusion | flops 676656640 | bytes 13773312 | tf_op jit(solution)/shard_map/hsid,hsjd->hsij/dot_general | solution.py:37
  124.7 17.5 %collective-permute-done.6 = bf16[2,10,512,128]{3,2,1,0:T(8,128)(2,1)} collective-permute-done((bf16[2,10,512,128]{3,2,1,0:T(8,128)(2,1)}, bf16[2,10,512,128]{3,2,1,0:T(8,128)(2,1)}, u32[]{:S(2)}, u32[]{:S(2)}) %collective-permute-start.6) | collective-permute-done | bytes 2621472 | tf_op jit(solution)/shard_map/ppermute | solution.py:14
  142.2 5.9 %maximum_select_fusion.1 = bf16[2,10,1024,128]{3,2,1,0:T(8,128)(2,1)S(1)} fusion(bf16[2,10,512,128]{3,2,1,0:T(8,128)(2,1)} %collective-permute-done.6, bf16[2,10,512,128]{3,2,1,0:T(8,128)(2,1)} %maximum_select_fusion.3, pred[]{:T(512)S(6)} %eq.64), kind=kLoop, calls=%fused_computation.14 | loop fusion | flops 23592960 | bytes 10485761 | tf_op jit(solution)/shard_map/jit(_where)/select_n | solution.py:52
  151.9 6.0 %exponential_reduce_fusion = f32[10,256]{1,0:T(8,128)S(1)} fusion(f32[10,256,1024]{2,1,0:T(8,128)} %get-tuple-element.47, f32[10,256]{1,0:T(8,128)S(1)} %select_bitcast_fusion.5), kind=kLoop, calls=%fused_computation.6 | loop fusion | flops 7861760 | bytes 10506240 | tf_op jit(solution)/shard_map/reduce_sum | solution.py:141
  168.4 15.3 %fusion.34 = f32[10,256,128]{1,2,0:T(8,128)S(1)} fusion(bf16[2,10,1024,128]{3,2,1,0:T(8,128)(2,1)} %copy-done.9, f32[10,256,1024]{2,1,0:T(8,128)} %get-tuple-element.47, f32[10,256]{1,0:T(8,128)S(1)} %select_bitcast_fusion.3, pred[10]{0:T(512)(128)(4,1)S(1)} %copy-done.47), kind=kOutput, calls=%fused_computation.98 | convolution fusion | flops 679280640 | bytes 14428170 | tf_op jit(solution)/shard_map/hsij,hsjd->hsid/dot_general | solution.py:148
  212.8 6.1 %convolution_bitcast_fusion.1 = f32[1,10,1024,128]{2,3,1,0:T(8,128)} fusion(f32[10,256,1024]{2,1,0:T(8,128)S(1)} %bitcast.334, f32[10,256]{1,0:T(8,128)S(1)} %copy-done.35, bf16[256,10,128]{2,0,1:T(8,128)(2,1)} %copy.113, pred[10]{0:T(512)(128)(4,1)S(1)} %copy-done.48), kind=kOutput, calls=%fused_computation.48 | convolution fusion | flops 679280640 | bytes 16394250 | tf_op jit(solution)/shard_map/hsij,hsid->hsjd/dot_general | solution.py:173
  226.8 4.9 collective-permute-start.14
  239.6 89.6 %collective-permute-done.23 = f32[2,10,64,128]{3,2,1,0:T(8,128)} collective-permute-done((f32[2,10,64,128]{3,2,1,0:T(8,128)S(1)}, f32[2,10,64,128]{3,2,1,0:T(8,128)}, u32[]{:S(2)}, u32[]{:S(2)}) %collective-permute-start.23) | collective-permute-done | bytes 655392 | tf_op jit(solution)/shard_map/ppermute | solution.py:14
  330.6 6.9 %select_add_fusion = f32[2,10,512,128]{2,3,1,0:T(8,128)S(1)} fusion(f32[2,10,512,128]{2,3,1,0:T(8,128)} %collective-permute-done.16, pred[]{:T(512)S(6)} %eq.76, f32[1,10,1024,128]{2,3,1,0:T(8,128)} %copy-done.2, f32[1,10,1024,128]{2,3,1,0:T(8,128)} %copy-done.3), kind=kLoop, calls=%fused_computation.17 | loop fusion | flops 5242880 | bytes 20971520 | tf_op jit(solution)/shard_map/add | solution.py:80
  341.0 4.9 fusion.33
  345.9 53.9 %collective-permute-done.24 = f32[2,10,32,128]{3,2,1,0:T(8,128)S(1)} collective-permute-done((f32[2,10,32,128]{3,2,1,0:T(8,128)S(1)}, f32[2,10,32,128]{3,2,1,0:T(8,128)S(1)}, u32[]{:S(2)}, u32[]{:S(2)}) %collective-permute-start.24) | collective-permute-done | bytes 327712 | tf_op jit(solution)/shard_map/ppermute | solution.py:14
  399.9 6.9 %collective-permute-start.25 = (f32[2,10,16,128]{3,2,1,0:T(8,128)S(1)}, f32[2,10,16,128]{3,2,1,0:T(8,128)S(1)}, u32[]{:S(2)}, u32[]{:S(2)}) collective-permute-start(f32[2,10,16,128]{3,2,1,0:T(8,128)S(1)} %slice_select_fusion.7), channel_id=1, source_target_pairs={{0,4},{1,5},{2,6},{3,7},{4,0},{5,1},{6,2},{7,3},{8,12},{9,13},{10,... | collective-permute-start | bytes 491528 | tf_op jit(solution)/shard_map/ppermute | solution.py:14
  416.8 4.1 select_add_fusion.2
  426.7 6.2 %collective-permute-start.15 = (f32[2,10,256,128]{2,3,1,0:T(8,128)}, f32[2,10,256,128]{2,3,1,0:T(8,128)}, u32[]{:S(2)}, u32[]{:S(2)}) collective-permute-start(f32[2,10,256,128]{2,3,1,0:T(8,128)} %slice_select_fusion.1), channel_id=1, source_target_pairs={{0,1},{1,0},{2,3},{3,2},{4,5},{5,4},{6,7},{7,6},{8,9},{9,8},{10,11... | collective-permute-start | bytes 7864328 | tf_op jit(solution)/shard_map/ppermute | solution.py:14
  434.3 13.6 %collective-permute-done.18 = f32[2,10,128,128]{2,3,1,0:T(8,128)S(1)} collective-permute-done((f32[2,10,128,128]{2,3,1,0:T(8,128)S(1)}, f32[2,10,128,128]{2,3,1,0:T(8,128)S(1)}, u32[]{:S(2)}, u32[]{:S(2)}) %collective-permute-start.18) | collective-permute-done | bytes 1310752 | tf_op jit(solution)/shard_map/ppermute | solution.py:14
  479.3 7.0 %collective-permute-start.20 = (f32[2,10,32,128]{3,2,1,0:T(8,128)S(1)}, f32[2,10,32,128]{3,2,1,0:T(8,128)S(1)}, u32[]{:S(2)}, u32[]{:S(2)}) collective-permute-start(f32[2,10,32,128]{3,2,1,0:T(8,128)S(1)} %copy.132), channel_id=1, source_target_pairs={{0,1},{1,0},{2,3},{3,2},{4,5},{5,4},{6,7},{7,6},{8,9},{9,8},{10,11... | collective-permute-start | bytes 983048 | tf_op jit(solution)/shard_map/ppermute | solution.py:14
  499.1 7.0 %fusion.27 = (bf16[256,1280]{0,1:T(8,128)(2,1)S(1)}, bf16[256,1280]{0,1:T(8,128)(2,1)}, bf16[256,1280]{0,1:T(8,128)(2,1)}, bf16[256,1280]{0,1:T(8,128)(2,1)}) fusion(f32[256,1280]{0,1:T(8,128)} %copy.141, f32[256,1280]{0,1:T(8,128)} %copy.143, f32[10,256,128]{1,2,0:T(8,128)} %get-tuple-element.24, pred[256,10]{0,1:T(8,128)(4,1)S(1)} %copy-done.37, ...), kind=kLoop, calls=%fused_computation.73 | loop fusion | flops 6553600 | bytes 18355200 | tf_op jit(solution)/shard_map/convert_element_type | solution.py:186
  (335 shorter events, 210.6 us)
Async XLA Ops:
  12.6 10.1 %collective-permute-start.7 = (bf16[2,10,4,128]{3,2,1,0:T(4,128)(2,1)S(1)}, bf16[2,10,4,128]{3,2,1,0:T(4,128)(2,1)S(1)}, u32[]{:S(2)}, u32[]{:S(2)}) collective-permute-start(bf16[2,10,4,128]{3,2,1,0:T(4,128)(2,1)S(1)} %pad_maximum_fusion.5), channel_id=1, source_target_pairs={{0,1},{1,0},{2,3},{3,2},{4,5},{5,4},{6,7},{7,6},{8,9},{9,8},{10,11... | collective-permute-start | bytes 61448 | tf_op jit(solution)/shard_map/ppermute | solution.py:14
  20.3 12.7 %collective-permute-start.3 = (bf16[2,10,64,128]{3,2,1,0:T(8,128)(2,1)S(1)}, bf16[2,10,64,128]{3,2,1,0:T(8,128)(2,1)S(1)}, u32[]{:S(2)}, u32[]{:S(2)}) collective-permute-start(bf16[2,10,64,128]{3,2,1,0:T(8,128)(2,1)S(1)} %maximum_select_fusion.9), channel_id=1, source_target_pairs={{0,2},{1,3},{2,0},{3,1},{4,6},{5,7},{6,4},{7,5},{8,10},{9,11},{10,... | collective-permute-start | bytes 983048 | tf_op jit(solution)/shard_map/ppermute | solution.py:14
  21.9 34.4 %collective-permute-start = (bf16[2,10,256,128]{3,2,1,0:T(8,128)(2,1)S(1)}, bf16[2,10,256,128]{3,2,1,0:T(8,128)(2,1)}, u32[]{:S(2)}, u32[]{:S(2)}) collective-permute-start(bf16[2,10,256,128]{3,2,1,0:T(8,128)(2,1)S(1)} %pad_maximum_fusion.3), channel_id=1, source_target_pairs={{0,1},{1,0},{2,3},{3,2},{4,5},{5,4},{6,7},{7,6},{8,9},{9,8},{10,11... | collective-permute-start | bytes 3932168 | tf_op jit(solution)/shard_map/ppermute | solution.py:14
  33.2 16.3 %collective-permute-start.4 = (bf16[2,10,128,128]{3,2,1,0:T(8,128)(2,1)S(1)}, bf16[2,10,128,128]{3,2,1,0:T(8,128)(2,1)}, u32[]{:S(2)}, u32[]{:S(2)}) collective-permute-start(bf16[2,10,128,128]{3,2,1,0:T(8,128)(2,1)S(1)} %maximum_select_fusion.7), channel_id=1, source_target_pairs={{0,4},{1,5},{2,6},{3,7},{4,0},{5,1},{6,2},{7,3},{8,12},{9,13},{10,... | collective-permute-start | bytes 1966088 | tf_op jit(solution)/shard_map/ppermute | solution.py:14
  41.1 12.8 %collective-permute-start.11 = (bf16[2,10,64,128]{3,2,1,0:T(8,128)(2,1)S(1)}, bf16[2,10,64,128]{3,2,1,0:T(8,128)(2,1)S(1)}, u32[]{:S(2)}, u32[]{:S(2)}) collective-permute-start(bf16[2,10,64,128]{3,2,1,0:T(8,128)(2,1)S(1)} %maximum_select_fusion.10), channel_id=1, source_target_pairs={{0,16},{1,17},{2,18},{3,19},{4,20},{5,21},{6,22},{7,23},{8,24},{9,... | collective-permute-start | bytes 983048 | tf_op jit(solution)/shard_map/ppermute | solution.py:14
  52.3 28.4 %collective-permute-start.5 = (bf16[2,10,256,128]{3,2,1,0:T(8,128)(2,1)}, bf16[2,10,256,128]{3,2,1,0:T(8,128)(2,1)}, u32[]{:S(2)}, u32[]{:S(2)}) collective-permute-start(bf16[2,10,256,128]{3,2,1,0:T(8,128)(2,1)} %maximum_select_fusion.5), channel_id=1, source_target_pairs={{0,8},{1,9},{2,10},{3,11},{4,12},{5,13},{6,14},{7,15},{8,0},{9,1},... | collective-permute-start | bytes 3932168 | tf_op jit(solution)/shard_map/ppermute | solution.py:14
  55.0 13.7 %collective-permute-start.12 = (bf16[2,10,128,128]{3,2,1,0:T(8,128)(2,1)}, bf16[2,10,128,128]{3,2,1,0:T(8,128)(2,1)}, u32[]{:S(2)}, u32[]{:S(2)}) collective-permute-start(bf16[2,10,128,128]{3,2,1,0:T(8,128)(2,1)} %maximum_select_fusion.8), channel_id=1, source_target_pairs={{0,32},{32,0},{64,96},{96,64},{1,33},{33,1},{65,97},{97,65},{2,34}... | collective-permute-start | bytes 1966088 | tf_op jit(solution)/shard_map/ppermute | solution.py:14
  59.4 55.4 %collective-permute-start.1 = (bf16[2,10,512,128]{3,2,1,0:T(8,128)(2,1)S(1)}, bf16[2,10,512,128]{3,2,1,0:T(8,128)(2,1)}, u32[]{:S(2)}, u32[]{:S(2)}) collective-permute-start(bf16[2,10,512,128]{3,2,1,0:T(8,128)(2,1)S(1)} %maximum_select_fusion.2), channel_id=1, source_target_pairs={{0,2},{1,3},{2,0},{3,1},{4,6},{5,7},{6,4},{7,5},{8,10},{9,11},{10,... | collective-permute-start | bytes 7864328 | tf_op jit(solution)/shard_map/ppermute | solution.py:14
  71.9 28.6 %collective-permute-start.13 = (bf16[2,10,256,128]{3,2,1,0:T(8,128)(2,1)}, bf16[2,10,256,128]{3,2,1,0:T(8,128)(2,1)}, u32[]{:S(2)}, u32[]{:S(2)}) collective-permute-start(bf16[2,10,256,128]{3,2,1,0:T(8,128)(2,1)} %maximum_select_fusion.6), channel_id=1, source_target_pairs={{0,64},{32,96},{64,0},{96,32},{1,65},{33,97},{65,1},{97,33},{2,66}... | collective-permute-start | bytes 3932168 | tf_op jit(solution)/shard_map/ppermute | solution.py:14
  85.0 57.3 %collective-permute-start.6 = (bf16[2,10,512,128]{3,2,1,0:T(8,128)(2,1)}, bf16[2,10,512,128]{3,2,1,0:T(8,128)(2,1)}, u32[]{:S(2)}, u32[]{:S(2)}) collective-permute-start(bf16[2,10,512,128]{3,2,1,0:T(8,128)(2,1)} %maximum_select_fusion.3), channel_id=1, source_target_pairs={{0,16},{1,17},{2,18},{3,19},{4,20},{5,21},{6,22},{7,23},{8,24},{9,... | collective-permute-start | bytes 7864328 | tf_op jit(solution)/shard_map/ppermute | solution.py:14
  190.8 28.1 %collective-permute-start.21 = (bf16[2,10,256,128]{3,2,1,0:T(8,128)(2,1)}, bf16[2,10,256,128]{3,2,1,0:T(8,128)(2,1)}, u32[]{:S(2)}, u32[]{:S(2)}) collective-permute-start(bf16[2,10,256,128]{3,2,1,0:T(8,128)(2,1)} %select_convert_fusion), channel_id=1, source_target_pairs={{0,64},{32,96},{64,0},{96,32},{1,65},{33,97},{65,1},{97,33},{2,66}... | collective-permute-start | bytes 3932168 | tf_op jit(solution)/shard_map/ppermute | solution.py:14
  203.2 127.4 %collective-permute-start.16 = (f32[2,10,512,128]{2,3,1,0:T(8,128)}, f32[2,10,512,128]{2,3,1,0:T(8,128)}, u32[]{:S(2)}, u32[]{:S(2)}) collective-permute-start(f32[2,10,512,128]{2,3,1,0:T(8,128)} %broadcast_select_fusion), channel_id=1, source_target_pairs={{0,16},{1,17},{2,18},{3,19},{4,20},{5,21},{6,22},{7,23},{8,24},{9,... | collective-permute-start | bytes 15728648 | tf_op jit(solution)/shard_map/ppermute | solution.py:14
  222.6 11.5 %collective-permute-start.22 = (bf16[2,10,128,128]{3,2,1,0:T(8,128)(2,1)S(1)}, bf16[2,10,128,128]{3,2,1,0:T(8,128)(2,1)S(1)}, u32[]{:S(2)}, u32[]{:S(2)}) collective-permute-start(bf16[2,10,128,128]{3,2,1,0:T(8,128)(2,1)S(1)} %select_convert_fusion.1), channel_id=1, source_target_pairs={{0,32},{32,0},{64,96},{96,64},{1,33},{33,1},{65,97},{97,65},{2,34}... | collective-permute-start | bytes 1966088 | tf_op jit(solution)/shard_map/ppermute | solution.py:14
  226.8 186.3 %collective-permute-start.14 = (f32[2,10,512,128]{2,3,1,0:T(8,128)}, f32[2,10,512,128]{2,3,1,0:T(8,128)}, u32[]{:S(2)}, u32[]{:S(2)}) collective-permute-start(f32[2,10,512,128]{2,3,1,0:T(8,128)} %broadcast_select_fusion.1), channel_id=1, source_target_pairs={{0,2},{1,3},{2,0},{3,1},{4,6},{5,7},{6,4},{7,5},{8,10},{9,11},{10,... | collective-permute-start | bytes 15728648 | tf_op jit(solution)/shard_map/ppermute | solution.py:14
  234.5 94.7 %collective-permute-start.23 = (f32[2,10,64,128]{3,2,1,0:T(8,128)S(1)}, f32[2,10,64,128]{3,2,1,0:T(8,128)}, u32[]{:S(2)}, u32[]{:S(2)}) collective-permute-start(f32[2,10,64,128]{3,2,1,0:T(8,128)S(1)} %slice_select_fusion.5), channel_id=1, source_target_pairs={{0,16},{1,17},{2,18},{3,19},{4,20},{5,21},{6,22},{7,23},{8,24},{9,... | collective-permute-start | bytes 1966088 | tf_op jit(solution)/shard_map/ppermute | solution.py:14
  339.4 77.5 %collective-permute-start.17 = (f32[2,10,256,128]{2,3,1,0:T(8,128)}, f32[2,10,256,128]{2,3,1,0:T(8,128)}, u32[]{:S(2)}, u32[]{:S(2)}) collective-permute-start(f32[2,10,256,128]{2,3,1,0:T(8,128)} %slice_select_fusion), channel_id=1, source_target_pairs={{0,8},{1,9},{2,10},{3,11},{4,12},{5,13},{6,14},{7,15},{8,0},{9,1},... | collective-permute-start | bytes 7864328 | tf_op jit(solution)/shard_map/ppermute | solution.py:14
  339.9 59.9 %collective-permute-start.24 = (f32[2,10,32,128]{3,2,1,0:T(8,128)S(1)}, f32[2,10,32,128]{3,2,1,0:T(8,128)S(1)}, u32[]{:S(2)}, u32[]{:S(2)}) collective-permute-start(f32[2,10,32,128]{3,2,1,0:T(8,128)S(1)} %slice_select_fusion.6), channel_id=1, source_target_pairs={{0,8},{1,9},{2,10},{3,11},{4,12},{5,13},{6,14},{7,15},{8,0},{9,1},... | collective-permute-start | bytes 983048 | tf_op jit(solution)/shard_map/ppermute | solution.py:14
  399.9 9.6 %collective-permute-start.25 = (f32[2,10,16,128]{3,2,1,0:T(8,128)S(1)}, f32[2,10,16,128]{3,2,1,0:T(8,128)S(1)}, u32[]{:S(2)}, u32[]{:S(2)}) collective-permute-start(f32[2,10,16,128]{3,2,1,0:T(8,128)S(1)} %slice_select_fusion.7), channel_id=1, source_target_pairs={{0,4},{1,5},{2,6},{3,7},{4,0},{5,1},{6,2},{7,3},{8,12},{9,13},{10,... | collective-permute-start | bytes 491528 | tf_op jit(solution)/shard_map/ppermute | solution.py:14
  409.6 24.6 %collective-permute-start.26 = (f32[2,10,8,128]{3,2,1,0:T(8,128)S(1)}, f32[2,10,8,128]{3,2,1,0:T(8,128)S(1)}, u32[]{:S(2)}, u32[]{:S(2)}) collective-permute-start(f32[2,10,8,128]{3,2,1,0:T(8,128)S(1)} %slice_select_fusion.8), channel_id=1, source_target_pairs={{0,2},{1,3},{2,0},{3,1},{4,6},{5,7},{6,4},{7,5},{8,10},{9,11},{10,... | collective-permute-start | bytes 245768 | tf_op jit(solution)/shard_map/ppermute | solution.py:14
  421.2 26.8 %collective-permute-start.18 = (f32[2,10,128,128]{2,3,1,0:T(8,128)S(1)}, f32[2,10,128,128]{2,3,1,0:T(8,128)S(1)}, u32[]{:S(2)}, u32[]{:S(2)}) collective-permute-start(f32[2,10,128,128]{2,3,1,0:T(8,128)S(1)} %slice_select_fusion.4), channel_id=1, source_target_pairs={{0,4},{1,5},{2,6},{3,7},{4,0},{5,1},{6,2},{7,3},{8,12},{9,13},{10,... | collective-permute-start | bytes 3932168 | tf_op jit(solution)/shard_map/ppermute | solution.py:14
  426.7 59.6 %collective-permute-start.15 = (f32[2,10,256,128]{2,3,1,0:T(8,128)}, f32[2,10,256,128]{2,3,1,0:T(8,128)}, u32[]{:S(2)}, u32[]{:S(2)}) collective-permute-start(f32[2,10,256,128]{2,3,1,0:T(8,128)} %slice_select_fusion.1), channel_id=1, source_target_pairs={{0,1},{1,0},{2,3},{3,2},{4,5},{5,4},{6,7},{7,6},{8,9},{9,8},{10,11... | collective-permute-start | bytes 7864328 | tf_op jit(solution)/shard_map/ppermute | solution.py:14
  434.2 35.6 %collective-permute-start.27 = (f32[2,10,4,128]{3,2,1,0:T(4,128)S(1)}, f32[2,10,4,128]{3,2,1,0:T(4,128)S(1)}, u32[]{:S(2)}, u32[]{:S(2)}) collective-permute-start(f32[2,10,4,128]{3,2,1,0:T(4,128)S(1)} %slice_select_fusion.9), channel_id=1, source_target_pairs={{0,1},{1,0},{2,3},{3,2},{4,5},{5,4},{6,7},{7,6},{8,9},{9,8},{10,11... | collective-permute-start | bytes 122888 | tf_op jit(solution)/shard_map/ppermute | solution.py:14
  452.2 22.0 %collective-permute-start.19 = (f32[2,10,64,128]{3,2,1,0:T(8,128)}, f32[2,10,64,128]{3,2,1,0:T(8,128)}, u32[]{:S(2)}, u32[]{:S(2)}) collective-permute-start(f32[2,10,64,128]{3,2,1,0:T(8,128)} %copy.130), channel_id=1, source_target_pairs={{0,2},{1,3},{2,0},{3,1},{4,6},{5,7},{6,4},{7,5},{8,10},{9,11},{10,... | collective-permute-start | bytes 1966088 | tf_op jit(solution)/shard_map/ppermute | solution.py:14
  479.3 12.6 %collective-permute-start.20 = (f32[2,10,32,128]{3,2,1,0:T(8,128)S(1)}, f32[2,10,32,128]{3,2,1,0:T(8,128)S(1)}, u32[]{:S(2)}, u32[]{:S(2)}) collective-permute-start(f32[2,10,32,128]{3,2,1,0:T(8,128)S(1)} %copy.132), channel_id=1, source_target_pairs={{0,1},{1,0},{2,3},{3,2},{4,5},{5,4},{6,7},{7,6},{8,9},{9,8},{10,11... | collective-permute-start | bytes 983048 | tf_op jit(solution)/shard_map/ppermute | solution.py:14
  (69 other events, 840.8 us)
where the time goes:
time: 523 us; the launch traced here: 513 us
  waiting for transfers between devices  218 us (42%)
  other arithmetic  94.9 us (18%)
  local copies, waits for them, and re-layouts  81.1 us (16%)
  starting transfers between devices  66.9 us (13%)
  matrix products  49.9 us (10%)
    ppermute x28, waiting for transfers between devices, swapped(): lax.ppermute(x, axis, [(i, i ^ 1 << distance) for i in range(lax.axis_siz...  218 us
    ppermute x28, starting transfers between devices, swapped(): lax.ppermute(x, axis, [(i, i ^ 1 << distance) for i in range(lax.axis_siz...  66.9 us
    broadcast_in_dim x37, local copies, waits for them, and re-layouts, spread(): placed = jnp.where(chosen, lifted[:, None], filler)  33.5 us
    unnamed x142, local copies, waits for them, and re-layouts  27.4 us
    add x14, other arithmetic, halve_step(): return kept_half + received_fn(outgoing)  26.3 us
    select_n x12, other arithmetic, lo_doubling(): jnp.where(is_lower, jnp.concatenate([pair_rows, partner], 2), jnp.concate...  24.1 us
    dot_general x3, matrix products, body(): jnp.einsum('hsij,hsjd->hsid', prob_b, sel_value, preferred_element_type=j...  19.2 us
    select_n x12, other arithmetic, halve_step(): outgoing = jnp.where(bit_on, lower_half, upper_half)  12.1 us
  transfers between devices with their start and end apart: 28, of which 14 were waited for; matrix products, arithmetic and copies ran while one was open for 27% of the time, Pallas kernels for 0%

commit v1 on v0

v1 whole, which is shorter than its diff:
```python
import functools

import jax
import jax.numpy as jnp
from jax import lax
from jax.experimental import pallas as pl
from jax.experimental.pallas import tpu as pltpu
from jax.sharding import PartitionSpec as P

H = 10
HD = 128
ROWS = 256
LOG2E = 1.4426950408889634
SCALING = HD ** -0.5
NEG = -1e30
VMEM_LIMIT = 48 * 1024 * 1024


def swapped(x, axis, mask):
    return lax.ppermute(x, axis, [(i, i ^ mask) for i in range(lax.axis_size(axis))])


def after(x, *others):
    return lax.optimization_barrier((x,) + others)[0]


def dot_nt(a, b):
    return lax.dot_general(a, b, (((1,), (1,)), ((), ())), preferred_element_type=jnp.float32)


def dot_nn(a, b):
    return lax.dot_general(a, b, (((1,), (0,)), ((), ())), preferred_element_type=jnp.float32)


def pick_kernel(off_ref, k_ref, v_ref, q_ref, g_ref, one_ref, two_ref):
    h = pl.program_id(0)
    i = lax.broadcasted_iota(jnp.int32, (48, ROWS), 0)
    p = lax.broadcasted_iota(jnp.int32, (48, ROWS), 1)
    target = jnp.where(i < 32, 8 * i + off_ref[1, h], 64 * (i - 32) + off_ref[2, h])
    onehot = (p == target).astype(jnp.bfloat16)
    for t, ref in enumerate((k_ref, v_ref, q_ref, g_ref)):
        rows = dot_nn(onehot, ref[...]).astype(jnp.bfloat16)
        one_ref[t] = rows[:32]
        two_ref[t] = rows[32:]


def pick(key, value, query, grad_out, offsets):
    column = pl.BlockSpec((ROWS, HD), lambda h, off: (0, h))
    return pl.pallas_call(
        pick_kernel,
        grid_spec=pltpu.PrefetchScalarGridSpec(
            num_scalar_prefetch=1,
            grid=(H,),
            in_specs=[column] * 4,
            out_specs=[
                pl.BlockSpec((4, 32, HD), lambda h, off: (0, 0, h)),
                pl.BlockSpec((4, 16, HD), lambda h, off: (0, 0, h)),
            ],
        ),
        out_shape=[
            jax.ShapeDtypeStruct((4, 32, H * HD), jnp.bfloat16),
            jax.ShapeDtypeStruct((4, 16, H * HD), jnp.bfloat16),
        ],
        cost_estimate=pl.CostEstimate(flops=2 * 48 * 256 * 128 * 40, bytes_accessed=3_400_000, transcendentals=0),
        name="pick_rows",
    )(offsets, key, value, query, grad_out)


def level_masks(off_ref, h):
    row = lax.broadcasted_iota(jnp.int32, (ROWS, 1), 0)
    return ((row & 7) == off_ref[1, h], (row & 63) == off_ref[2, h])


def forward_kernel(off_ref, q_ref, g_ref, *refs):
    k_refs, v_refs, (att_ref, dq_ref, stat_ref) = refs[:8], refs[8:16], refs[16:]
    h = pl.program_id(0)
    sel1, sel2 = level_masks(off_ref, h)
    masks = [None] * 4 + [sel1] * 2 + [sel2] * 2
    q = q_ref[...]
    g = g_ref[...]
    keys = [r[...].reshape(-1, HD) for r in k_refs]
    values = [r[...].reshape(-1, HD) for r in v_refs]
    scores = []
    for k, mask in zip(keys, masks):
        s = dot_nt(q, k) * (SCALING * LOG2E)
        scores.append(s if mask is None else jnp.where(mask, s, NEG))
    peak = functools.reduce(jnp.maximum, [jnp.max(s, 1, keepdims=True) for s in scores])
    exps = [jnp.exp2(s - peak) for s in scores]
    total = sum(jnp.sum(e, 1, keepdims=True) for e in exps)
    inv = 1.0 / total
    probs = [e * inv for e in exps]
    out = sum(dot_nn(p.astype(jnp.bfloat16), v) for p, v in zip(probs, values))
    att_ref[...] = out.astype(jnp.bfloat16)
    row_dot = jnp.sum(out * g.astype(jnp.float32), 1, keepdims=True)
    dq = jnp.zeros((ROWS, HD), jnp.float32)
    for p, k, v in zip(probs, keys, values):
        ds = (p * (dot_nt(g, v) - row_dot)).astype(jnp.bfloat16)
        dq = dq + dot_nn(ds, k)
    dq_ref[...] = (dq * SCALING).astype(jnp.bfloat16)
    lse = peak + jnp.log2(total)
    i = lax.broadcasted_iota(jnp.int32, (ROWS, 384), 0)
    j = lax.broadcasted_iota(jnp.int32, (ROWS, 384), 1)
    target = jnp.where(j < 256, j, jnp.where(j < 288, 8 * (j - 256) + off_ref[1, h], 64 * (j - 288) + off_ref[2, h]))
    hit = i == target
    stat_ref[0] = jnp.concatenate(
        [jnp.sum(jnp.where(hit, x, 0.0), 0, keepdims=True) for x in (lse, row_dot)], 0
    )


def backward_kernel(off_ref, k_ref, v_ref, *refs):
    q_refs, g_refs, s_refs, (dk_ref, dv_ref) = refs[:8], refs[8:16], refs[16:24], refs[24:]
    h = pl.program_id(0)
    sel1, sel2 = level_masks(off_ref, h)
    masks = [None] * 4 + [sel1] * 2 + [sel2] * 2
    k = k_ref[...]
    v = v_ref[...]
    dk = jnp.zeros((ROWS, HD), jnp.float32)
    dv = jnp.zeros((ROWS, HD), jnp.float32)
    for q_ref, g_ref, s_ref, mask in zip(q_refs, g_refs, s_refs, masks):
        q = q_ref[...].reshape(-1, HD)
        g = g_ref[...].reshape(-1, HD)
        lse = s_ref[0, 0:1, : q.shape[0]]
        row_dot = s_ref[0, 1:2, : q.shape[0]]
        s = dot_nt(k, q) * (SCALING * LOG2E) - lse
        if mask is not None:
            s = jnp.where(mask, s, NEG)
        p = jnp.exp2(s)
        ds = (p * (dot_nt(v, g) - row_dot)).astype(jnp.bfloat16)
        dv = dv + dot_nn(p.astype(jnp.bfloat16), g)
        dk = dk + dot_nn(ds, q)
    dk_ref[...] = (dk * SCALING).astype(jnp.bfloat16)
    dv_ref[...] = dv.astype(jnp.bfloat16)


COLUMN = pl.BlockSpec((ROWS, HD), lambda h, off: (0, h))


def one_spec(t):
    return pl.BlockSpec((4, 4, 1, 32, HD), lambda h, off: (0, 0, t, 0, h))


def two_spec(t):
    return pl.BlockSpec((4, 4, 1, 16, HD), lambda h, off: (0, 0, t, 0, h))


def stat_spec(width):
    return pl.BlockSpec((1, 2, width), lambda h, off: (h, 0, 0))


PARAMS = pltpu.CompilerParams(vmem_limit_bytes=VMEM_LIMIT)
COST = pl.CostEstimate(flops=2 * 256 * 2560 * 128 * 40, bytes_accessed=15_000_000, transcendentals=256 * 2560 * 10)


def forward(offsets, q, g, k0, v0, one, two):
    wide = jax.ShapeDtypeStruct((ROWS, H * HD), jnp.bfloat16)
    return pl.pallas_call(
        forward_kernel,
        grid_spec=pltpu.PrefetchScalarGridSpec(
            num_scalar_prefetch=1,
            grid=(H,),
            in_specs=[COLUMN] * 2
            + [COLUMN] * 4 + [one_spec(0)] * 2 + [two_spec(0)] * 2
            + [COLUMN] * 4 + [one_spec(1)] * 2 + [two_spec(1)] * 2,
            out_specs=[COLUMN, COLUMN, stat_spec(384)],
        ),
        out_shape=[wide, wide, jax.ShapeDtypeStruct((H, 2, 384), jnp.float32)],
        compiler_params=PARAMS,
        cost_estimate=COST,
        name="forward",
    )(offsets, q, g, *k0, *one, *two, *v0, *one, *two)


def backward(offsets, k, v, q0, g0, one, two, s0, s1, s2):
    wide = jax.ShapeDtypeStruct((ROWS, H * HD), jnp.bfloat16)
    return pl.pallas_call(
        backward_kernel,
        grid_spec=pltpu.PrefetchScalarGridSpec(
            num_scalar_prefetch=1,
            grid=(H,),
            in_specs=[COLUMN] * 2
            + [COLUMN] * 4 + [one_spec(0)] * 2 + [two_spec(2)] * 2
            + [COLUMN] * 4 + [one_spec(1)] * 2 + [two_spec(3)] * 2
            + [stat_spec(384)] * 4 + [stat_spec(512)] * 2 + [stat_spec(256)] * 2,
            out_specs=[COLUMN, COLUMN],
        ),
        out_shape=[wide, wide],
        compiler_params=PARAMS,
        cost_estimate=COST,
        name="backward",
    )(offsets, k, v, *q0, *one, *two, *g0, *one, *two, *s0, *s1, *s2)


CORE, XS, ZS, YS = 1, (2, 4, 6), (8, 16, 24), (1, 2, 3)


def around(x, axis, masks):
    return [x] + [swapped(x, axis, m) for m in masks]


def body(query, key, value, grad_out, offsets):
    kx = swapped(key, "seqlo", XS[0])
    one, two = pick(key, value, query, grad_out, offsets)
    two = two[:, :4]

    two = jnp.concatenate(around(two, "seqlo", XS), 1)
    two = jnp.stack(around(two, "seqlo", ZS))
    two = jnp.stack(around(two, "seqhi", YS))
    two_c = swapped(two, "seqlo", CORE)

    one_a = jnp.stack(around(one[:2], "seqlo", XS))
    one_b = jnp.stack(around(one[2:], "seqlo", XS))
    vx = swapped(after(value, one_a), "seqlo", XS[0])
    full_a = jnp.stack(around(one_a, "seqlo", ZS))
    full_b = jnp.stack(around(after(one_b, full_a), "seqlo", ZS))
    full_ac = swapped(full_a, "seqlo", CORE)
    full_bc = swapped(full_b, "seqlo", CORE)

    qx = swapped(after(query, kx), "seqlo", XS[0])
    gx = swapped(after(grad_out, vx), "seqlo", XS[0])
    kc, vc, qc, gc, kxc, vxc, qxc, gxc = [
        swapped(t, "seqlo", CORE) for t in (key, value, query, grad_out, kx, vx, qx, gx)
    ]

    attended, grad_query, stats = forward(
        offsets, query, grad_out, [key, kc, kx, kxc], [value, vc, vx, vxc], [full_a, full_ac], [two, two_c]
    )

    sx = swapped(stats, "seqlo", XS[0])
    sc = swapped(stats, "seqlo", CORE)
    sxc = swapped(sx, "seqlo", CORE)
    small = stats[:, :, 256:]
    small = jnp.stack([small, sx[:, :, 256:]] + [swapped(small, "seqlo", m) for m in XS[1:]])
    small = jnp.stack(around(small, "seqlo", ZS))
    small_c = swapped(small, "seqlo", CORE)
    tiny = small[..., 32:36].transpose(2, 3, 0, 1, 4).reshape(H * 2, 64)
    tiny = jnp.stack(around(tiny, "seqhi", YS), 1).reshape(H, 2, 256)
    tiny_c = swapped(tiny, "seqlo", CORE)
    s1 = [t[..., :32].transpose(2, 3, 0, 1, 4).reshape(H, 2, 512) for t in (small, small_c)]

    grad_key, grad_value = backward(
        offsets, key, value, [query, qc, qx, qxc], [grad_out, gc, gx, gxc],
        [full_b, full_bc], [two, two_c], [stats, sc, sx, sxc], s1, [tiny, tiny_c],
    )
    return attended, grad_query, grad_key, grad_value


def solution(mesh):
    spec = P(("seqhi", "seqlo"), None)
    return jax.shard_map(
        body,
        mesh=mesh,
        in_specs=(spec, spec, spec, spec, P()),
        out_specs=(spec, spec, spec, spec),
        check_vma=False,
    )
```

time: 523 us -> 259 us (0.50); the launches traced: 513 us -> 258 us
  waiting for transfers between devices: 218 us -> 102 us
  other arithmetic: 94.9 us -> 4.42 us
  local copies, waits for them, and re-layouts: 81.1 us -> 12.7 us
  Pallas kernels: 0 us -> 60.5 us
  matrix products: 49.9 us -> 0 us
  starting transfers between devices: 66.9 us -> 77.3 us
    ppermute x28 -> x49, waiting for transfers between devices: 218 us -> 102 us  [swapped(): lax.ppermute(x, axis, [(i, i ^ mask) for i in range(lax.axis_size(axis))])]
    pallas_call x0 -> x3, Pallas kernels: none -> 60.5 us  [the longest x1 29 us: forward(): pl.pallas_call(forward_kernel, grid_spec=pltpu.PrefetchScalarGridSpec(num...]
    dot_general x18 -> x0, matrix products: 49.9 us -> none  [the longest x3 19.2 us: body(): jnp.einsum('hsij,hsjd->hsid', prob_b, sel_value, preferred_element_type=j...]
    select_n x30 -> x0, other arithmetic: 44.9 us -> none  [the longest x12 24.1 us: lo_doubling(): jnp.where(is_lower, jnp.concatenate([pair_rows, partner], 2), jnp.concate...]
    broadcast_in_dim x37 -> x0, local copies, waits for them, and re-layouts: 33.5 us -> none  [spread(): placed = jnp.where(chosen, lifted[:, None], filler)]
    add x14 -> x0, other arithmetic: 26.3 us -> none  [halve_step(): return kept_half + received_fn(outgoing)]
    unnamed x142 -> x20, local copies, waits for them, and re-layouts: 27.4 us -> 3.06 us
    reduce_sum x11 -> x0, other arithmetic: 13.9 us -> none  [the longest x7 7.04 us: pick(): jnp.sum(jnp.where(chosen, grouped, jnp.zeros((), source.dtype)), axis=1)]
  transfers between devices with their start and end apart: 28 -> 49, of which waited for: 14 -> 16; matrix products, arithmetic and copies ran while one was open for 27% -> 5% of each run, Pallas kernels for 0% -> 11%
where the time goes in v1:
time: 259 us; the launch traced here: 258 us
  waiting for transfers between devices  102 us (39%)
  starting transfers between devices  77.3 us (30%)
  Pallas kernels  60.5 us (23%)
  local copies, waits for them, and re-layouts  12.7 us (5%)
  other arithmetic  4.42 us (2%)
    ppermute x49, waiting for transfers between devices, swapped(): lax.ppermute(x, axis, [(i, i ^ mask) for i in range(lax.axis_size(axis))])  102 us
    ppermute x49, starting transfers between devices, swapped(): lax.ppermute(x, axis, [(i, i ^ mask) for i in range(lax.axis_size(axis))])  77.3 us
    pallas_call x1, Pallas kernels, forward(): pl.pallas_call(forward_kernel, grid_spec=pltpu.PrefetchScalarGridSpec(num...  29 us
    pallas_call x1, Pallas kernels, backward(): pl.pallas_call(backward_kernel, grid_spec=pltpu.PrefetchScalarGridSpec(nu...  23.8 us
    pallas_call x1, Pallas kernels, pick(): pl.pallas_call(pick_kernel, grid_spec=pltpu.PrefetchScalarGridSpec(num_sc...  7.69 us
  transfers between devices with their start and end apart: 49, of which 16 were waited for; matrix products, arithmetic and copies ran while one was open for 5% of the time, Pallas kernels for 11%

profile of v1, /device:TPU:1, one launch (start us, length us, event | category | flops | bytes accessed | tf_op | source)
XLA Modules:
  0.0 258.4 jit_solution(17068356981999346881)
XLA Ops:
  0.6 7.7 %pick_rows.1 = (bf16[4,32,1280]{2,1,0:T(8,128)(2,1)}, bf16[4,16,1280]{2,1,0:T(8,128)(2,1)}) custom-call(s32[3,10]{1,0:T(4,128)} %off_ref.5, bf16[256,1280]{1,0:T(8,128)(2,1)} %k_ref.3, bf16[256,1280]{1,0:T(8,128)(2,1)} %v_ref.3, bf16[256,1280]{1,0:T(8,128)(2,1)} %refs_0_.3, bf16[256,1280]{1,0:T(8,128)(2,1)} %refs_8_.3), custom_call_target="tpu_custom_call" | custom-call | flops 125829120 | bytes 3400000 | tf_op jit(solution)/shard_map/pick_rows/pallas_call | solution.py:49
  9.4 3.4 %collective-permute-start.5 = (bf16[2,32,1280]{2,1,0:T(8,128)(2,1)S(1)}, bf16[2,32,1280]{2,1,0:T(8,128)(2,1)S(1)}, u32[]{:S(2)}, u32[]{:S(2)}) collective-permute-start(bf16[2,32,1280]{2,1,0:T(8,128)(2,1)S(1)} %get-tuple-element.33), channel_id=1, source_target_pairs={{0,6},{1,7},{2,4},{3,5},{4,2},{5,3},{6,0},{7,1},{8,14},{9,15},{10,... | collective-permute-start | bytes 491528 | tf_op jit(solution)/shard_map/ppermute | solution.py:20
  14.3 2.7 %collective-permute-start.12 = (bf16[4,4,1280]{2,1,0:T(4,128)(2,1)S(1)}, bf16[4,4,1280]{2,1,0:T(4,128)(2,1)S(1)}, u32[]{:S(2)}, u32[]{:S(2)}) collective-permute-start(bf16[4,4,1280]{2,1,0:T(4,128)(2,1)S(1)} %slice.25), channel_id=1, source_target_pairs={{0,6},{1,7},{2,4},{3,5},{4,2},{5,3},{6,0},{7,1},{8,14},{9,15},{10,... | collective-permute-start | bytes 122888 | tf_op jit(solution)/shard_map/ppermute | solution.py:20
  20.4 4.0 %collective-permute-start.8 = (bf16[4,2,32,1280]{3,2,1,0:T(8,128)(2,1)S(1)}, bf16[4,2,32,1280]{3,2,1,0:T(8,128)(2,1)S(1)}, u32[]{:S(2)}, u32[]{:S(2)}) collective-permute-start(bf16[4,2,32,1280]{3,2,1,0:T(8,128)(2,1)S(1)} %get-tuple-element.29), channel_id=1, source_target_pairs={{0,24},{1,25},{2,26},{3,27},{4,28},{5,29},{6,30},{7,31},{8,16},{9,... | collective-permute-start | bytes 1966088 | tf_op jit(solution)/shard_map/ppermute | solution.py:20
  30.2 28.0 %collective-permute-done.15 = bf16[4,16,1280]{2,1,0:T(8,128)(2,1)S(1)} collective-permute-done((bf16[4,16,1280]{2,1,0:T(8,128)(2,1)S(1)}, bf16[4,16,1280]{2,1,0:T(8,128)(2,1)S(1)}, u32[]{:S(2)}, u32[]{:S(2)}) %collective-permute-start.15) | collective-permute-done | bytes 163872 | tf_op jit(solution)/shard_map/ppermute | solution.py:20
  58.3 2.8 %collective-permute-start.18 = (bf16[4,4,16,1280]{3,2,1,0:T(8,128)(2,1)S(1)}, bf16[4,4,16,1280]{3,2,1,0:T(8,128)(2,1)S(1)}, u32[]{:S(2)}, u32[]{:S(2)}) collective-permute-start(bf16[4,4,16,1280]{3,2,1,0:T(8,128)(2,1)S(1)} %get-tuple-element.27), channel_id=1, source_target_pairs={{0,96},{32,64},{64,32},{96,0},{1,97},{33,65},{65,33},{97,1},{2,98}... | collective-permute-start | bytes 1966088 | tf_op jit(solution)/shard_map/ppermute | solution.py:20
  61.8 9.7 %collective-permute-done.6 = bf16[4,2,32,1280]{3,2,1,0:T(8,128)(2,1)S(1)} collective-permute-done((bf16[4,2,32,1280]{3,2,1,0:T(8,128)(2,1)S(1)}, bf16[4,2,32,1280]{3,2,1,0:T(8,128)(2,1)S(1)}, u32[]{:S(2)}, u32[]{:S(2)}) %collective-permute-start.6) | collective-permute-done | bytes 655392 | tf_op jit(solution)/shard_map/ppermute | solution.py:20
  71.9 3.9 %collective-permute-start.9 = (bf16[4,4,2,32,1280]{4,3,2,1,0:T(8,128)(2,1)S(1)}, bf16[4,4,2,32,1280]{4,3,2,1,0:T(8,128)(2,1)S(1)}, u32[]{:S(2)}, u32[]{:S(2)}) collective-permute-start(bf16[4,4,2,32,1280]{4,3,2,1,0:T(8,128)(2,1)S(1)} %pad_maximum_fusion.refs_4_.refs_12_), channel_id=1, source_target_pairs={{0,1},{1,0},{2,3},{3,2},{4,5},{5,4},{6,7},{7,6},{8,9},{9,8},{10,11... | collective-permute-start | bytes 7864328 | tf_op jit(solution)/shard_map/ppermute | solution.py:20
  75.8 13.4 %collective-permute-done.18 = bf16[4,4,16,1280]{3,2,1,0:T(8,128)(2,1)S(1)} collective-permute-done((bf16[4,4,16,1280]{3,2,1,0:T(8,128)(2,1)S(1)}, bf16[4,4,16,1280]{3,2,1,0:T(8,128)(2,1)S(1)}, u32[]{:S(2)}, u32[]{:S(2)}) %collective-permute-start.18) | collective-permute-done | bytes 655392 | tf_op jit(solution)/shard_map/ppermute | solution.py:20
  92.0 3.5 %collective-permute-start.28 = (bf16[2,32,1280]{2,1,0:T(8,128)(2,1)S(1)}, bf16[2,32,1280]{2,1,0:T(8,128)(2,1)S(1)}, u32[]{:S(2)}, u32[]{:S(2)}) collective-permute-start(bf16[2,32,1280]{2,1,0:T(8,128)(2,1)S(1)} %get-tuple-element.32), channel_id=1, source_target_pairs={{0,6},{1,7},{2,4},{3,5},{4,2},{5,3},{6,0},{7,1},{8,14},{9,15},{10,... | collective-permute-start | bytes 491528 | tf_op jit(solution)/shard_map/ppermute | solution.py:20
  97.2 5.3 %collective-permute-done.28 = bf16[2,32,1280]{2,1,0:T(8,128)(2,1)S(1)} collective-permute-done((bf16[2,32,1280]{2,1,0:T(8,128)(2,1)S(1)}, bf16[2,32,1280]{2,1,0:T(8,128)(2,1)S(1)}, u32[]{:S(2)}, u32[]{:S(2)}) %collective-permute-start.28) | collective-permute-done | bytes 163872 | tf_op jit(solution)/shard_map/ppermute | solution.py:20
  104.0 2.7 %collective-permute-done.26 = bf16[2,32,1280]{2,1,0:T(8,128)(2,1)S(1)} collective-permute-done((bf16[2,32,1280]{2,1,0:T(8,128)(2,1)S(1)}, bf16[2,32,1280]{2,1,0:T(8,128)(2,1)S(1)}, u32[]{:S(2)}, u32[]{:S(2)}) %collective-permute-start.26) | collective-permute-done | bytes 163872 | tf_op jit(solution)/shard_map/ppermute | solution.py:20
  109.9 10.8 %collective-permute-done.1.refs_2_ = bf16[256,1280]{1,0:T(8,128)(2,1)S(1)} collective-permute-done((bf16[256,1280]{1,0:T(8,128)(2,1)S(1)}, bf16[256,1280]{1,0:T(8,128)(2,1)S(1)}, u32[]{:S(2)}, u32[]{:S(2)}) %collective-permute-start.1) | collective-permute-done | bytes 655392 | tf_op jit(solution)/shard_map/ppermute | solution.py:20
  120.7 3.6 %collective-permute-start.30 = (bf16[4,2,32,1280]{3,2,1,0:T(8,128)(2,1)S(1)}, bf16[4,2,32,1280]{3,2,1,0:T(8,128)(2,1)S(1)}, u32[]{:S(2)}, u32[]{:S(2)}) collective-permute-start(bf16[4,2,32,1280]{3,2,1,0:T(8,128)(2,1)S(1)} %pad_maximum_fusion.5), channel_id=1, source_target_pairs={{0,16},{1,17},{2,18},{3,19},{4,20},{5,21},{6,22},{7,23},{8,24},{9,... | collective-permute-start | bytes 1966088 | tf_op jit(solution)/shard_map/ppermute | solution.py:20
  124.3 10.5 %collective-permute-done.21.refs_10_ = bf16[256,1280]{1,0:T(8,128)(2,1)S(1)} collective-permute-done((bf16[256,1280]{1,0:T(8,128)(2,1)S(1)}, bf16[256,1280]{1,0:T(8,128)(2,1)S(1)}, u32[]{:S(2)}, u32[]{:S(2)}) %collective-permute-start.21) | collective-permute-done | bytes 655392 | tf_op jit(solution)/shard_map/ppermute | solution.py:20
  136.2 2.8 %collective-permute-start.20 = (bf16[256,1280]{1,0:T(8,128)(2,1)S(1)}, bf16[256,1280]{1,0:T(8,128)(2,1)S(1)}, u32[]{:S(2)}, u32[]{:S(2)}) collective-permute-start(bf16[256,1280]{1,0:T(8,128)(2,1)S(1)} %copy-done.3), channel_id=1, source_target_pairs={{0,1},{1,0},{2,3},{3,2},{4,5},{5,4},{6,7},{7,6},{8,9},{9,8},{10,11... | collective-permute-start | bytes 1966088 | tf_op jit(solution)/shard_map/ppermute | solution.py:20
  141.2 10.3 %collective-permute-done.29 = bf16[4,2,32,1280]{3,2,1,0:T(8,128)(2,1)S(1)} collective-permute-done((bf16[4,2,32,1280]{3,2,1,0:T(8,128)(2,1)S(1)}, bf16[4,2,32,1280]{3,2,1,0:T(8,128)(2,1)S(1)}, u32[]{:S(2)}, u32[]{:S(2)}) %collective-permute-start.29) | collective-permute-done | bytes 655392 | tf_op jit(solution)/shard_map/ppermute | solution.py:20
  160.1 29.0 %forward.1 = (bf16[256,1280]{1,0:T(8,128)(2,1)}, bf16[256,1280]{1,0:T(8,128)(2,1)}, f32[10,2,384]{2,1,0:T(2,128)S(1)}) custom-call(s32[3,10]{1,0:T(4,128)S(1)} %copy-done.4, bf16[256,1280]{1,0:T(8,128)(2,1)S(1)} %copy-done, bf16[256,1280]{1,0:T(8,128)(2,1)S(1)} %copy-done.1, bf16[256,1280]{1,0:T(8,128)(2,1)S(1)} %copy-done.2, ...), custom_call_target="tpu_custom_call" | custom-call | flops 6710886400 | bytes 15000000 | tf_op jit(solution)/shard_map/forward/pallas_call | solution.py:156
  189.6 3.8 %collective-permute-start.40 = (f32[10,2,128]{2,1,0:T(2,128)S(1)}, f32[10,2,128]{2,1,0:T(2,128)S(1)}, u32[]{:S(2)}, u32[]{:S(2)}) collective-permute-start(f32[10,2,128]{2,1,0:T(2,128)S(1)} %get-tuple-element.37), channel_id=1, source_target_pairs={{0,6},{1,7},{2,4},{3,5},{4,2},{5,3},{6,0},{7,1},{8,14},{9,15},{10,... | collective-permute-start | bytes 30728 | tf_op jit(solution)/shard_map/ppermute | solution.py:20
  196.6 2.7 %collective-permute-start.39 = (f32[10,2,128]{2,1,0:T(2,128)S(1)}, f32[10,2,128]{2,1,0:T(2,128)S(1)}, u32[]{:S(2)}, u32[]{:S(2)}) collective-permute-start(f32[10,2,128]{2,1,0:T(2,128)S(1)} %get-tuple-element.37), channel_id=1, source_target_pairs={{0,4},{1,5},{2,6},{3,7},{4,0},{5,1},{6,2},{7,3},{8,12},{9,13},{10,... | collective-permute-start | bytes 30728 | tf_op jit(solution)/shard_map/ppermute | solution.py:20
  201.7 2.9 %collective-permute-start.42 = (f32[4,10,2,128]{3,2,1,0:T(2,128)S(1)}, f32[4,10,2,128]{3,2,1,0:T(2,128)S(1)}, u32[]{:S(2)}, u32[]{:S(2)}) collective-permute-start(f32[4,10,2,128]{3,2,1,0:T(2,128)S(1)} %pad_maximum_fusion.9), channel_id=1, source_target_pairs={{0,16},{1,17},{2,18},{3,19},{4,20},{5,21},{6,22},{7,23},{8,24},{9,... | collective-permute-start | bytes 122888 | tf_op jit(solution)/shard_map/ppermute | solution.py:20
  212.4 2.7 %collective-permute-start.47 = (f32[20,64]{1,0:T(8,128)S(1)}, f32[20,64]{1,0:T(8,128)}, u32[]{:S(2)}, u32[]{:S(2)}) collective-permute-start(f32[20,64]{1,0:T(8,128)S(1)} %reshape.22), channel_id=1, source_target_pairs={{0,96},{32,64},{64,32},{96,0},{1,97},{33,65},{65,33},{97,1},{2,98}... | collective-permute-start | bytes 15368 | tf_op jit(solution)/shard_map/ppermute | solution.py:20
  223.2 3.5 %collective-permute-start.44 = (f32[4,4,10,2,128]{4,3,2,1,0:T(2,128)}, f32[4,4,10,2,128]{4,3,2,1,0:T(2,128)}, u32[]{:S(2)}, u32[]{:S(2)}) collective-permute-start(f32[4,4,10,2,128]{4,3,2,1,0:T(2,128)} %pad_maximum_fusion.7), channel_id=1, source_target_pairs={{0,1},{1,0},{2,3},{3,2},{4,5},{5,4},{6,7},{7,6},{8,9},{9,8},{10,11... | collective-permute-start | bytes 491528 | tf_op jit(solution)/shard_map/ppermute | solution.py:20
  234.5 23.8 %backward.1 = (bf16[256,1280]{1,0:T(8,128)(2,1)}, bf16[256,1280]{1,0:T(8,128)(2,1)}) custom-call(s32[3,10]{1,0:T(4,128)S(1)} %copy-done.4, bf16[256,1280]{1,0:T(8,128)(2,1)S(1)} %copy-done.2, bf16[256,1280]{1,0:T(8,128)(2,1)S(1)} %copy-done.3, bf16[256,1280]{1,0:T(8,128)(2,1)S(1)} %copy-done, bf16[256,1280]{1,0:T(8,128)(2,1)} %collective-permute-done.23.refs_1_, ...), custom_call_target="tpu_custom_call" | custom-call | flops 6710886400 | bytes 15000000 | tf_op jit(solution)/shard_map/backward/pallas_call | solution.py:175
  (124 shorter events, 64.0 us)
Async XLA Ops:
  20.4 41.1 %collective-permute-start.8 = (bf16[4,2,32,1280]{3,2,1,0:T(8,128)(2,1)S(1)}, bf16[4,2,32,1280]{3,2,1,0:T(8,128)(2,1)S(1)}, u32[]{:S(2)}, u32[]{:S(2)}) collective-permute-start(bf16[4,2,32,1280]{3,2,1,0:T(8,128)(2,1)S(1)} %get-tuple-element.29), channel_id=1, source_target_pairs={{0,24},{1,25},{2,26},{3,27},{4,28},{5,29},{6,30},{7,31},{8,16},{9,... | collective-permute-start | bytes 1966088 | tf_op jit(solution)/shard_map/ppermute | solution.py:20
  24.5 33.7 %collective-permute-start.15 = (bf16[4,16,1280]{2,1,0:T(8,128)(2,1)S(1)}, bf16[4,16,1280]{2,1,0:T(8,128)(2,1)S(1)}, u32[]{:S(2)}, u32[]{:S(2)}) collective-permute-start(bf16[4,16,1280]{2,1,0:T(8,128)(2,1)S(1)} %get-tuple-element.35), channel_id=1, source_target_pairs={{0,24},{1,25},{2,26},{3,27},{4,28},{5,29},{6,30},{7,31},{8,16},{9,... | collective-permute-start | bytes 491528 | tf_op jit(solution)/shard_map/ppermute | solution.py:20
  27.1 31.1 %collective-permute-start.14 = (bf16[4,16,1280]{2,1,0:T(8,128)(2,1)S(1)}, bf16[4,16,1280]{2,1,0:T(8,128)(2,1)S(1)}, u32[]{:S(2)}, u32[]{:S(2)}) collective-permute-start(bf16[4,16,1280]{2,1,0:T(8,128)(2,1)S(1)} %get-tuple-element.35), channel_id=1, source_target_pairs={{0,16},{1,17},{2,18},{3,19},{4,20},{5,21},{6,22},{7,23},{8,24},{9,... | collective-permute-start | bytes 491528 | tf_op jit(solution)/shard_map/ppermute | solution.py:20
  27.1 31.1 %collective-permute-start.13 = (bf16[4,16,1280]{2,1,0:T(8,128)(2,1)S(1)}, bf16[4,16,1280]{2,1,0:T(8,128)(2,1)S(1)}, u32[]{:S(2)}, u32[]{:S(2)}) collective-permute-start(bf16[4,16,1280]{2,1,0:T(8,128)(2,1)S(1)} %get-tuple-element.35), channel_id=1, source_target_pairs={{0,8},{1,9},{2,10},{3,11},{4,12},{5,13},{6,14},{7,15},{8,0},{9,1},... | collective-permute-start | bytes 491528 | tf_op jit(solution)/shard_map/ppermute | solution.py:20
  27.8 34.0 %collective-permute-start.7 = (bf16[4,2,32,1280]{3,2,1,0:T(8,128)(2,1)S(1)}, bf16[4,2,32,1280]{3,2,1,0:T(8,128)(2,1)S(1)}, u32[]{:S(2)}, u32[]{:S(2)}) collective-permute-start(bf16[4,2,32,1280]{3,2,1,0:T(8,128)(2,1)S(1)} %get-tuple-element.29), channel_id=1, source_target_pairs={{0,16},{1,17},{2,18},{3,19},{4,20},{5,21},{6,22},{7,23},{8,24},{9,... | collective-permute-start | bytes 1966088 | tf_op jit(solution)/shard_map/ppermute | solution.py:20
  58.3 30.9 %collective-permute-start.18 = (bf16[4,4,16,1280]{3,2,1,0:T(8,128)(2,1)S(1)}, bf16[4,4,16,1280]{3,2,1,0:T(8,128)(2,1)S(1)}, u32[]{:S(2)}, u32[]{:S(2)}) collective-permute-start(bf16[4,4,16,1280]{3,2,1,0:T(8,128)(2,1)S(1)} %get-tuple-element.27), channel_id=1, source_target_pairs={{0,96},{32,64},{64,32},{96,0},{1,97},{33,65},{65,33},{97,1},{2,98}... | collective-permute-start | bytes 1966088 | tf_op jit(solution)/shard_map/ppermute | solution.py:20
  61.2 28.0 %collective-permute-start.17 = (bf16[4,4,16,1280]{3,2,1,0:T(8,128)(2,1)S(1)}, bf16[4,4,16,1280]{3,2,1,0:T(8,128)(2,1)S(1)}, u32[]{:S(2)}, u32[]{:S(2)}) collective-permute-start(bf16[4,4,16,1280]{3,2,1,0:T(8,128)(2,1)S(1)} %get-tuple-element.27), channel_id=1, source_target_pairs={{0,64},{32,96},{64,0},{96,32},{1,65},{33,97},{65,1},{97,33},{2,66}... | collective-permute-start | bytes 1966088 | tf_op jit(solution)/shard_map/ppermute | solution.py:20
  61.5 27.7 %collective-permute-start.16 = (bf16[4,4,16,1280]{3,2,1,0:T(8,128)(2,1)S(1)}, bf16[4,4,16,1280]{3,2,1,0:T(8,128)(2,1)S(1)}, u32[]{:S(2)}, u32[]{:S(2)}) collective-permute-start(bf16[4,4,16,1280]{3,2,1,0:T(8,128)(2,1)S(1)} %get-tuple-element.27), channel_id=1, source_target_pairs={{0,32},{32,0},{64,96},{96,64},{1,33},{33,1},{65,97},{97,65},{2,34}... | collective-permute-start | bytes 1966088 | tf_op jit(solution)/shard_map/ppermute | solution.py:20
  71.9 85.2 %collective-permute-start.9 = (bf16[4,4,2,32,1280]{4,3,2,1,0:T(8,128)(2,1)S(1)}, bf16[4,4,2,32,1280]{4,3,2,1,0:T(8,128)(2,1)S(1)}, u32[]{:S(2)}, u32[]{:S(2)}) collective-permute-start(bf16[4,4,2,32,1280]{4,3,2,1,0:T(8,128)(2,1)S(1)} %pad_maximum_fusion.refs_4_.refs_12_), channel_id=1, source_target_pairs={{0,1},{1,0},{2,3},{3,2},{4,5},{5,4},{6,7},{7,6},{8,9},{9,8},{10,11... | collective-permute-start | bytes 7864328 | tf_op jit(solution)/shard_map/ppermute | solution.py:20
  89.6 69.0 %collective-permute-start.19 = (bf16[4,4,4,16,1280]{4,3,2,1,0:T(8,128)(2,1)S(1)}, bf16[4,4,4,16,1280]{4,3,2,1,0:T(8,128)(2,1)S(1)}, u32[]{:S(2)}, u32[]{:S(2)}) collective-permute-start(bf16[4,4,4,16,1280]{4,3,2,1,0:T(8,128)(2,1)S(1)} %pad_maximum_fusion.1.refs_6_.refs_14_), channel_id=1, source_target_pairs={{0,1},{1,0},{2,3},{3,2},{4,5},{5,4},{6,7},{7,6},{8,9},{9,8},{10,11... | collective-permute-start | bytes 7864328 | tf_op jit(solution)/shard_map/ppermute | solution.py:20
  103.2 17.5 %collective-permute-start.1 = (bf16[256,1280]{1,0:T(8,128)(2,1)S(1)}, bf16[256,1280]{1,0:T(8,128)(2,1)S(1)}, u32[]{:S(2)}, u32[]{:S(2)}) collective-permute-start(bf16[256,1280]{1,0:T(8,128)(2,1)S(1)} %copy-done.2), channel_id=1, source_target_pairs={{0,2},{1,3},{2,0},{3,1},{4,6},{5,7},{6,4},{7,5},{8,10},{9,11},{10,... | collective-permute-start | bytes 1966088 | tf_op jit(solution)/shard_map/ppermute | solution.py:20
  106.7 28.0 %collective-permute-start.21 = (bf16[256,1280]{1,0:T(8,128)(2,1)S(1)}, bf16[256,1280]{1,0:T(8,128)(2,1)S(1)}, u32[]{:S(2)}, u32[]{:S(2)}) collective-permute-start(bf16[256,1280]{1,0:T(8,128)(2,1)S(1)} %copy-done.3), channel_id=1, source_target_pairs={{0,2},{1,3},{2,0},{3,1},{4,6},{5,7},{6,4},{7,5},{8,10},{9,11},{10,... | collective-permute-start | bytes 1966088 | tf_op jit(solution)/shard_map/ppermute | solution.py:20
  107.4 28.8 %collective-permute-start.31 = (bf16[4,2,32,1280]{3,2,1,0:T(8,128)(2,1)S(1)}, bf16[4,2,32,1280]{3,2,1,0:T(8,128)(2,1)S(1)}, u32[]{:S(2)}, u32[]{:S(2)}) collective-permute-start(bf16[4,2,32,1280]{3,2,1,0:T(8,128)(2,1)S(1)} %pad_maximum_fusion.5), channel_id=1, source_target_pairs={{0,24},{1,25},{2,26},{3,27},{4,28},{5,29},{6,30},{7,31},{8,16},{9,... | collective-permute-start | bytes 1966088 | tf_op jit(solution)/shard_map/ppermute | solution.py:20
  120.7 18.3 %collective-permute-start.30 = (bf16[4,2,32,1280]{3,2,1,0:T(8,128)(2,1)S(1)}, bf16[4,2,32,1280]{3,2,1,0:T(8,128)(2,1)S(1)}, u32[]{:S(2)}, u32[]{:S(2)}) collective-permute-start(bf16[4,2,32,1280]{3,2,1,0:T(8,128)(2,1)S(1)} %pad_maximum_fusion.5), channel_id=1, source_target_pairs={{0,16},{1,17},{2,18},{3,19},{4,20},{5,21},{6,22},{7,23},{8,24},{9,... | collective-permute-start | bytes 1966088 | tf_op jit(solution)/shard_map/ppermute | solution.py:20
  134.7 16.8 %collective-permute-start.29 = (bf16[4,2,32,1280]{3,2,1,0:T(8,128)(2,1)S(1)}, bf16[4,2,32,1280]{3,2,1,0:T(8,128)(2,1)S(1)}, u32[]{:S(2)}, u32[]{:S(2)}) collective-permute-start(bf16[4,2,32,1280]{3,2,1,0:T(8,128)(2,1)S(1)} %pad_maximum_fusion.5), channel_id=1, source_target_pairs={{0,8},{1,9},{2,10},{3,11},{4,12},{5,13},{6,14},{7,15},{8,0},{9,1},... | collective-permute-start | bytes 1966088 | tf_op jit(solution)/shard_map/ppermute | solution.py:20
  136.2 19.1 %collective-permute-start.20 = (bf16[256,1280]{1,0:T(8,128)(2,1)S(1)}, bf16[256,1280]{1,0:T(8,128)(2,1)S(1)}, u32[]{:S(2)}, u32[]{:S(2)}) collective-permute-start(bf16[256,1280]{1,0:T(8,128)(2,1)S(1)} %copy-done.3), channel_id=1, source_target_pairs={{0,1},{1,0},{2,3},{3,2},{4,5},{5,4},{6,7},{7,6},{8,9},{9,8},{10,11... | collective-permute-start | bytes 1966088 | tf_op jit(solution)/shard_map/ppermute | solution.py:20
  139.0 16.3 %collective-permute-start.2 = (bf16[256,1280]{1,0:T(8,128)(2,1)S(1)}, bf16[256,1280]{1,0:T(8,128)(2,1)S(1)}, u32[]{:S(2)}, u32[]{:S(2)}) collective-permute-start(bf16[256,1280]{1,0:T(8,128)(2,1)S(1)} %collective-permute-done.1.refs_2_), channel_id=1, source_target_pairs={{0,1},{1,0},{2,3},{3,2},{4,5},{5,4},{6,7},{7,6},{8,9},{9,8},{10,11... | collective-permute-start | bytes 1966088 | tf_op jit(solution)/shard_map/ppermute | solution.py:20
  155.3 79.2 %collective-permute-start.32 = (bf16[4,4,2,32,1280]{4,3,2,1,0:T(8,128)(2,1)}, bf16[4,4,2,32,1280]{4,3,2,1,0:T(8,128)(2,1)}, u32[]{:S(2)}, u32[]{:S(2)}) collective-permute-start(bf16[4,4,2,32,1280]{4,3,2,1,0:T(8,128)(2,1)} %pad_maximum_fusion.2.refs_4_.refs_12_), channel_id=1, source_target_pairs={{0,1},{1,0},{2,3},{3,2},{4,5},{5,4},{6,7},{7,6},{8,9},{9,8},{10,11... | collective-permute-start | bytes 7864328 | tf_op jit(solution)/shard_map/ppermute | solution.py:20
  155.3 46.4 %collective-permute-start.24 = (bf16[256,1280]{1,0:T(8,128)(2,1)S(1)}, bf16[256,1280]{1,0:T(8,128)(2,1)S(1)}, u32[]{:S(2)}, u32[]{:S(2)}) collective-permute-start(bf16[256,1280]{1,0:T(8,128)(2,1)S(1)} %copy-done), channel_id=1, source_target_pairs={{0,2},{1,3},{2,0},{3,1},{4,6},{5,7},{6,4},{7,5},{8,10},{9,11},{10,... | collective-permute-start | bytes 1966088 | tf_op jit(solution)/shard_map/ppermute | solution.py:20
  155.8 48.8 %collective-permute-start.34 = (bf16[256,1280]{1,0:T(8,128)(2,1)S(1)}, bf16[256,1280]{1,0:T(8,128)(2,1)}, u32[]{:S(2)}, u32[]{:S(2)}) collective-permute-start(bf16[256,1280]{1,0:T(8,128)(2,1)S(1)} %copy-done.1), channel_id=1, source_target_pairs={{0,2},{1,3},{2,0},{3,1},{4,6},{5,7},{6,4},{7,5},{8,10},{9,11},{10,... | collective-permute-start | bytes 1966088 | tf_op jit(solution)/shard_map/ppermute | solution.py:20
  194.5 17.9 %collective-permute-start.23 = (bf16[256,1280]{1,0:T(8,128)(2,1)S(1)}, bf16[256,1280]{1,0:T(8,128)(2,1)}, u32[]{:S(2)}, u32[]{:S(2)}) collective-permute-start(bf16[256,1280]{1,0:T(8,128)(2,1)S(1)} %copy-done), channel_id=1, source_target_pairs={{0,1},{1,0},{2,3},{3,2},{4,5},{5,4},{6,7},{7,6},{8,9},{9,8},{10,11... | collective-permute-start | bytes 1966088 | tf_op jit(solution)/shard_map/ppermute | solution.py:20
  204.8 26.2 %collective-permute-start.33 = (bf16[256,1280]{1,0:T(8,128)(2,1)S(1)}, bf16[256,1280]{1,0:T(8,128)(2,1)}, u32[]{:S(2)}, u32[]{:S(2)}) collective-permute-start(bf16[256,1280]{1,0:T(8,128)(2,1)S(1)} %copy-done.1), channel_id=1, source_target_pairs={{0,1},{1,0},{2,3},{3,2},{4,5},{5,4},{6,7},{7,6},{8,9},{9,8},{10,11... | collective-permute-start | bytes 1966088 | tf_op jit(solution)/shard_map/ppermute | solution.py:20
  207.1 24.0 %collective-permute-start.25 = (bf16[256,1280]{1,0:T(8,128)(2,1)S(1)}, bf16[256,1280]{1,0:T(8,128)(2,1)}, u32[]{:S(2)}, u32[]{:S(2)}) collective-permute-start(bf16[256,1280]{1,0:T(8,128)(2,1)S(1)} %collective-permute-done.24.refs_2_), channel_id=1, source_target_pairs={{0,1},{1,0},{2,3},{3,2},{4,5},{5,4},{6,7},{7,6},{8,9},{9,8},{10,11... | collective-permute-start | bytes 1966088 | tf_op jit(solution)/shard_map/ppermute | solution.py:20
  209.0 25.5 %collective-permute-start.35 = (bf16[256,1280]{1,0:T(8,128)(2,1)}, bf16[256,1280]{1,0:T(8,128)(2,1)}, u32[]{:S(2)}, u32[]{:S(2)}) collective-permute-start(bf16[256,1280]{1,0:T(8,128)(2,1)} %collective-permute-done.34.refs_10_), channel_id=1, source_target_pairs={{0,1},{1,0},{2,3},{3,2},{4,5},{5,4},{6,7},{7,6},{8,9},{9,8},{10,11... | collective-permute-start | bytes 1966088 | tf_op jit(solution)/shard_map/ppermute | solution.py:20
  (35 other events, 281.1 us)
